TPU v7x, 32 devices: a whole 2x2x4 slice. The times are simulated.
32 devices in a mesh: ctx: 8 (over z, x), tp: 4 (over y, core).
Axes of the slice: x: 2, y: 2, z: 4, core: 2. Of those that a mesh axis runs over, the one named last changes fastest.
Arguments:
- queries: bfloat16 [1024, 1024], P('ctx', 'tp'), may hold values from -5 to 5
- key_states: bfloat16 [1024, 1024], P('ctx', 'tp'), may hold values from -5 to 5
- value_states: bfloat16 [1024, 1024], P('ctx', 'tp'), may hold values from -6 to 6
- attn_output: bfloat16 [1024, 1024], P('ctx', 'tp'), may hold values from -6 to 6
- output_grad: bfloat16 [1024, 1024], P('ctx', 'tp'), may hold values from -6 to 6
- block_map: int32 [8, 8], replicated, may hold values from 0 to 1, as said below
- w_query: bfloat16 [8192, 1024], P('ctx', 'tp'), may hold values from -0.1875 to 0.1875
- w_key: bfloat16 [8192, 1024], P('ctx', 'tp'), may hold values from -0.1875 to 0.1875
- w_value: bfloat16 [8192, 1024], P('ctx', 'tp'), may hold values from -0.1875 to 0.1875
Outputs:
- grad_input: bfloat16 [1024, 8192], P('tp', 'ctx')
Inputs may be any that keep to these rules, and one draw needn't show every extreme that they name: block_map[i, j] is 1 wherever |i - j| <= 1; elsewhere each row is 1 on a share of its entries that differs from row to row.
All inputs are finite; a program needn't handle non-finite values.
Results may differ from a plain program's by a relative error of at most 0.014.
Values may be sent and summed in bfloat16 or wider, within the bound.
A program may use at most 64 MiB of HBM per device.

v0:
```python
import math

import jax
import jax.numpy as jnp
from jax import lax
from jax.sharding import PartitionSpec as P

HD = 128
BLK = 128


NEG_FILL = -1e30


def block_mask(block_map, row_offset, row_count, col_offset, col_count):
    tiles = lax.dynamic_slice(
        block_map, (row_offset // BLK, col_offset // BLK), (row_count // BLK, col_count // BLK)
    )
    spread = jnp.broadcast_to(
        tiles[:, None, :, None], (row_count // BLK, BLK, col_count // BLK, BLK)
    )
    return spread.reshape(row_count, col_count) > 0


def resolved_rows(values):
    return lax.optimization_barrier(values.astype(jnp.bfloat16)).astype(jnp.float32)


def stat_update(state, query_heads, key_block, allowed, score_scale):
    row_max, row_sum = state
    scores = (
        jnp.einsum("qhd,khd->hqk", query_heads, key_block, preferred_element_type=jnp.float32)
        * score_scale
    )
    masked = jnp.where(allowed[None], scores, NEG_FILL)
    new_max = jnp.maximum(row_max, jnp.max(masked, axis=2))
    kept = jnp.where(allowed[None], jnp.exp(masked - new_max[:, :, None]), 0.0)
    return (new_max, row_sum * jnp.exp(row_max - new_max) + jnp.sum(kept, axis=2))


def gradient_block(
    query_heads, grad_heads, key_block, value_block, log_total, row_delta, allowed, score_scale
):
    scores = (
        jnp.einsum("qhd,khd->hqk", query_heads, key_block, preferred_element_type=jnp.float32)
        * score_scale
    )
    masked = jnp.where(allowed[None], scores, NEG_FILL)
    probs = jnp.where(allowed[None], jnp.exp(masked - log_total[:, :, None]), 0.0)
    probs_low = probs.astype(jnp.bfloat16)
    dprobs = jnp.einsum("qhd,khd->hqk", grad_heads, value_block, preferred_element_type=jnp.float32)
    score_gradient = (probs * (dprobs - row_delta[:, :, None]) * score_scale).astype(jnp.bfloat16)
    return (probs_low, score_gradient)


def per_device(
    queries, key_states, value_states, attn_output, output_grad, block_map, w_query, w_key, w_value
):
    slab_rows, width = queries.shape
    head_count = width // HD
    context_count = lax.axis_size("ctx")
    score_scale = 1.0 / math.sqrt(HD)
    row_offset = lax.axis_index("ctx") * slab_rows
    query_heads = queries.reshape(slab_rows, head_count, HD)
    grad_heads = output_grad.reshape(slab_rows, head_count, HD)
    output_heads = attn_output.reshape(slab_rows, head_count, HD)
    row_delta = jnp.sum(grad_heads.astype(jnp.float32) * output_heads.astype(jnp.float32), axis=2).T
    start_state = (
        jnp.full((head_count, slab_rows), NEG_FILL, jnp.float32),
        jnp.zeros((head_count, slab_rows), jnp.float32),
    )
    full_keys, full_values = (
        lax.all_gather(key_states, "ctx", axis=0, tiled=True),
        lax.all_gather(value_states, "ctx", axis=0, tiled=True),
    )
    group_size = min(context_count, max(1, 512 // slab_rows))
    key_span = slab_rows * group_size
    total_block_count = context_count // group_size
    key_blocks = full_keys.reshape(total_block_count, key_span, head_count, HD)
    value_blocks = full_values.reshape(total_block_count, key_span, head_count, HD)
    block_ids = jnp.arange(total_block_count, dtype=jnp.int32)

    def stat_step(state, inputs):
        key_block, block_index = inputs
        allowed = block_mask(block_map, row_offset, slab_rows, block_index * key_span, key_span)

        def stat_active_step(previous):
            return stat_update(previous, query_heads, key_block, allowed, score_scale)

        return (
            lax.cond(jnp.any(allowed), stat_active_step, lambda previous: previous, state),
            None,
        )

    (row_max, row_sum), _ = lax.scan(stat_step, start_state, (key_blocks, block_ids))
    log_total = row_max + jnp.log(row_sum)

    def back_step(dq_total, inputs):
        key_block, value_block, block_index = inputs
        allowed = block_mask(block_map, row_offset, slab_rows, block_index * key_span, key_span)

        def back_active_step(previous):
            probs_low, score_gradient = gradient_block(
                query_heads,
                grad_heads,
                key_block,
                value_block,
                log_total,
                row_delta,
                allowed,
                score_scale,
            )
            dv_part = jnp.einsum(
                "hqk,qhd->khd", probs_low, grad_heads, preferred_element_type=jnp.float32
            ).astype(jnp.bfloat16)
            dk_part = jnp.einsum(
                "hqk,qhd->khd", score_gradient, query_heads, preferred_element_type=jnp.float32
            ).astype(jnp.bfloat16)
            per_slab = jnp.einsum(
                "hqgk,gkhd->gqhd",
                score_gradient.reshape(head_count, slab_rows, group_size, slab_rows),
                key_block.reshape(group_size, slab_rows, head_count, HD),
                preferred_element_type=jnp.float32,
            )
            joined = jnp.concatenate(
                [dk_part.reshape(key_span, width), dv_part.reshape(key_span, width)], axis=1
            )
            return (previous + jnp.sum(resolved_rows(per_slab), axis=0), joined)

        def empty_step(previous):
            return (previous, jnp.zeros((key_span, 2 * width), jnp.bfloat16))

        return lax.cond(jnp.any(allowed), back_active_step, empty_step, dq_total)

    dq_total, joined_blocks = lax.scan(
        back_step,
        jnp.zeros((slab_rows, head_count, HD), jnp.float32),
        (key_blocks, value_blocks, block_ids),
    )
    local_grads = dq_total.astype(jnp.bfloat16).reshape(slab_rows, width)
    part_grads = joined_blocks.reshape(context_count * slab_rows, 2 * width)
    part_width = part_grads.shape[1]
    arrived = lax.all_to_all(
        part_grads.reshape(context_count, slab_rows, part_width),
        "ctx",
        split_axis=0,
        concat_axis=0,
        tiled=True,
    )
    finished = jnp.sum(arrived.astype(jnp.float32), axis=0).astype(jnp.bfloat16)
    own_grads = jnp.concatenate([local_grads, finished], axis=1)
    gradients = lax.all_gather(own_grads, "ctx", axis=0, tiled=True)
    projections = jnp.concatenate([w_query, w_key, w_value], axis=1)
    return lax.psum_scatter(
        lax.dot_general(
            gradients, projections, (((1,), (1,)), ((), ())), preferred_element_type=jnp.float32
        ).astype(jnp.bfloat16),
        "tp",
        scatter_dimension=0,
        tiled=True,
    )


def solution(mesh):
    return jax.shard_map(
        per_device,
        mesh=mesh,
        in_specs=(
            P("ctx", "tp"),
            P("ctx", "tp"),
            P("ctx", "tp"),
            P("ctx", "tp"),
            P("ctx", "tp"),
            P(),
            P("ctx", "tp"),
            P("ctx", "tp"),
            P("ctx", "tp"),
        ),
        out_specs=P("tp", "ctx"),
        check_vma=False,
    )
```

profile of v0, /device:TPU:0, one launch (start us, length us, event | category | flops | bytes accessed | tf_op | source)
XLA Modules:
  0.0 200.5 jit_solution(11003897744795206140)
XLA Ops:
  6.5 0.9 copy.62
  7.5 1.0 copy.59
  8.5 0.1 copy.61
  8.6 0.9 copy.63
  9.5 33.2 %all_gather.9 = bf16[1024,256]{1,0:T(8,128)(2,1)S(1)} all-gather(bf16[128,256]{1,0:T(8,128)(2,1)} %param.18), channel_id=1, replica_groups=mesh['ctx'=8,'tp'=4] {'ctx'}, dimensions={0}, use_global_device_ids=true | all-gather | bytes 589824 | tf_op jit(solution)/shard_map/all_gather | solution.py:73
  42.8 0.1 reshape.78
  42.9 0.1 copy.64
  43.0 7.4 %while.33 = (s32[]{:T(128)}, f32[2,128]{1,0:T(2,128)S(1)}, f32[2,128]{1,0:T(2,128)S(1)}, s32[2]{0:T(128)S(1)}, s32[8,8]{1,0:T(8,128)}, /*index=5*/s32[]{:T(128)}...) while((s32[]{:T(128)}, f32[2,128]{1,0:T(2,128)S(1)}, ...), condition=%wide.region_6.7_spmd, body=%wide.region_0.6_spmd.sunk | while | flops 34406940 | bytes 1391631 | solution.py:95
  43.0 0.7 dynamic_slice.72
  44.3 0.8 broadcast_compare_fusion.6
  45.1 0.7 broadcast_reduce_fusion.4
  46.4 0.5 conditional.4
  46.5 0.1 broadcast_bitcast_fusion
  46.5 0.3 fusion.26
  46.8 0.2 select_reduce_fusion
  47.0 0.7 dynamic_slice.72
  48.3 0.8 broadcast_compare_fusion.6
  49.1 0.7 broadcast_reduce_fusion.4
  50.4 31.3 %all_gather.10 = bf16[1024,256]{1,0:T(8,128)(2,1)S(1)} all-gather(bf16[128,256]{1,0:T(8,128)(2,1)S(1)} %copy-done), channel_id=1, replica_groups=mesh['ctx'=8,'tp'=4] {'ctx'}, dimensions={0}, use_global_device_ids=true | all-gather | bytes 589824 | tf_op jit(solution)/shard_map/all_gather | solution.py:74
  81.7 0.1 reshape.80
  81.9 0.1 copy.65
  82.0 10.7 %while.34 = (s32[]{:T(128)}, f32[128,2,128]{2,0,1:T(8,128)S(1)}, bf16[2,512,512]{2,1,0:T(8,128)(2,1)}, s32[2]{0:T(128)S(1)}, s32[8,8]{1,0:T(8,128)}, /*index=5*/...) while((s32[]{:T(128)}, f32[128,2,128]{2,0,1:T(8,128)S(1)}, ...), condition=%wide.region_13.14_spmd, body=%wide.region_8.13_spmd.sunk | while | flops 170721312 | bytes 8654899 | solution.py:135
  82.0 0.6 dynamic_slice.73
  83.3 0.8 broadcast_compare_fusion.7
  84.1 0.8 broadcast_reduce_fusion.5
  85.5 1.5 conditional.5
  85.6 0.1 broadcast_bitcast_fusion.1
  85.7 0.3 fusion.10
  85.9 0.2 fusion.11
  86.2 0.2 convolution_convert_fusion
  86.4 0.3 fusion.12
  86.8 0.2 convolution_convert_fusion.1
  87.0 0.2 copy.81
  87.3 0.8 constant_dynamic-update-slice_fusion.2
  88.1 0.6 dynamic_slice.73
  89.4 0.8 broadcast_compare_fusion.7
  90.1 0.8 broadcast_reduce_fusion.5
  91.6 0.2 copy.81
  91.9 0.8 constant_dynamic-update-slice_fusion.2
  92.7 5.8 %all-to-all-start = ((bf16[8,128,512]{2,1,0:T(8,128)(2,1)}), bf16[8,128,512]{2,1,0:T(8,128)(2,1)S(1)}, u32[]{:S(2)}, u32[]{:S(2)}) async-start(bf16[8,128,512]{2,1,0:T(8,128)(2,1)} %bitcast.24), calls=%async_computation | async-start | bytes 2097152 | tf_op jit(solution)/shard_map/all_to_all | solution.py:143
  98.5 0.1 copy.66
  98.7 0.1 copy.68
  98.8 16.1 %all-to-all-done = bf16[8,128,512]{2,1,0:T(8,128)(2,1)S(1)} async-done(((bf16[8,128,512]{2,1,0:T(8,128)(2,1)}), bf16[8,128,512]{2,1,0:T(8,128)(2,1)S(1)}, u32[]{:S(2)}, u32[]{:S(2)}) %all-to-all-start) | async-done | bytes 1048608 | tf_op jit(solution)/shard_map/all_to_all | solution.py:143
  114.8 0.1 reduce_sum.43
  115.0 0.7 pad_maximum_fusion
  115.8 42.9 %all-gather.2.cloned.1.call-done = bf16[1024,768]{1,0:T(8,128)(2,1)} async-done(((bf16[128,768]{1,0:T(8,128)(2,1)}), bf16[1024,768]{1,0:T(8,128)(2,1)}) %all-gather.2.cloned.1.call-update) | async-done | bytes 1572880 | tf_op jit(solution)/shard_map/all_gather | solution.py:152
  158.7 4.6 %convolution_convert_fusion.3 = bf16[1024,1024]{1,0:T(8,128)(2,1)} fusion(bf16[1024,768]{1,0:T(8,128)(2,1)} %all-gather.2.cloned.1.call-done, bf16[1024,256]{1,0:T(8,128)(2,1)S(1)} %copy-done.1, bf16[1024,256]{1,0:T(8,128)(2,1)S(1)} %copy-done.2, bf16[1024,256]{1,0:T(8,128)(2,1)S(1)} %copy-done.3), kind=kOutput, calls=%fused_computation.42 | convolution fusion | flops 1616379904 | bytes 5242880 | tf_op jit(solution)/shard_map/dot_general | solution.py:155
  163.3 30.4 %reduce-scatter.2.cloned.1.call-done = bf16[256,1024]{1,0:T(8,128)(2,1)} async-done(((bf16[1024,1024]{1,0:T(8,128)(2,1)}), bf16[256,1024]{1,0:T(8,128)(2,1)}) %reduce-scatter.2.cloned.1.call-update) | async-done | bytes 524304 | tf_op jit(solution)/shard_map/reduce_scatter | solution.py:154
  (32 shorter events, 0.5 us)
Async XLA Ops:
  43.0 7.4 %copy-start = (bf16[128,256]{1,0:T(8,128)(2,1)S(1)}, bf16[128,256]{1,0:T(8,128)(2,1)}, u32[]{:S(2)}) copy-start(bf16[128,256]{1,0:T(8,128)(2,1)} %param.19) | copy-start | bytes 196612
  92.7 22.1 %all-to-all-start = ((bf16[8,128,512]{2,1,0:T(8,128)(2,1)}), bf16[8,128,512]{2,1,0:T(8,128)(2,1)S(1)}, u32[]{:S(2)}, u32[]{:S(2)}) async-start(bf16[8,128,512]{2,1,0:T(8,128)(2,1)} %bitcast.24), calls=%async_computation | async-start | bytes 2097152 | tf_op jit(solution)/shard_map/all_to_all | solution.py:143
  98.5 60.2 %copy-start.1 = (bf16[1024,256]{1,0:T(8,128)(2,1)S(1)}, bf16[1024,256]{1,0:T(8,128)(2,1)}, u32[]{:S(2)}) copy-start(bf16[1024,256]{1,0:T(8,128)(2,1)} %param.25) | copy-start | bytes 1572868
  98.5 60.2 %copy-start.2 = (bf16[1024,256]{1,0:T(8,128)(2,1)S(1)}, bf16[1024,256]{1,0:T(8,128)(2,1)}, u32[]{:S(2)}) copy-start(bf16[1024,256]{1,0:T(8,128)(2,1)} %param.24) | copy-start | bytes 1572868
  98.5 60.2 %copy-start.3 = (bf16[1024,256]{1,0:T(8,128)(2,1)S(1)}, bf16[1024,256]{1,0:T(8,128)(2,1)}, u32[]{:S(2)}) copy-start(bf16[1024,256]{1,0:T(8,128)(2,1)} %param.23) | copy-start | bytes 1572868
  98.5 60.2 %all-gather.2.cloned.1.call-start = ((), (), s32[]{:S(2)}) async-start(), calls=%async_computation.2 | async-start | bytes 1769472 | tf_op jit(solution)/shard_map/all_gather | solution.py:152
  115.7 78.0 %reduce-scatter.2.cloned.1.call-start = ((), (), s32[]{:S(2)}) async-start(), calls=%async_computation.3 | async-start | bytes 2621440 | tf_op jit(solution)/shard_map/reduce_scatter | solution.py:154
Sparse Core Ops, SparseCore 0:
  115.8 42.8 all-gather.1
  163.4 30.2 reduce-scatter.1
where the time goes:
time: 202 us; the launch traced here: 201 us
  waiting for transfers between devices  89.4 us (44%)
  blocking collectives  64.5 us (32%)
  between operations  13.6 us (7%)
  local copies, waits for them, and re-layouts  8.45 us (4%)
  other arithmetic  7.33 us (4%)
  matrix products  6.06 us (3%)
  starting transfers between devices  5.83 us (3%)
  loops' own time  5.34 us (3%)
    all_gather x1, waiting for transfers between devices, per_device(): gradients = lax.all_gather(own_grads, 'ctx', axis=0, tiled=True)  42.9 us
    all_gather x1, blocking collectives, per_device(): lax.all_gather(key_states, 'ctx', axis=0, tiled=True)  33.2 us
    all_gather x1, blocking collectives, per_device(): lax.all_gather(value_states, 'ctx', axis=0, tiled=True)  31.3 us
    reduce_scatter x1, waiting for transfers between devices, per_device(): lax.psum_scatter(lax.dot_general(gradients, projections, (((1,), (1,)), (...  30.4 us
    all_to_all x1, waiting for transfers between devices, per_device(): lax.all_to_all(part_grads.reshape(context_count, slab_rows, part_width),...  16.1 us
    all_to_all x1, starting transfers between devices, per_device(): lax.all_to_all(part_grads.reshape(context_count, slab_rows, part_width),...  5.75 us
    dot_general x1, matrix products, per_device(): lax.dot_general(gradients, projections, (((1,), (1,)), ((), ())), preferr...  4.58 us
  transfers between devices with their start and end apart: 3, of which 3 were waited for; matrix products, arithmetic and copies ran while one was open for 0% of the time, Pallas kernels for 0%

commit v1 on v0

--- a/solution.py
+++ b/solution.py
@@ -1,8 +1,11 @@
+import functools
 import math
 
 import jax
 import jax.numpy as jnp
 from jax import lax
+from jax.experimental import pallas as pl
+from jax.experimental.pallas import tpu as pltpu
 from jax.sharding import PartitionSpec as P
 
 HD = 128
@@ -161,9 +164,374 @@
     )
 
 
+MESH = pl.DeviceIdType.MESH
+LOG2E = 1.4426950408889634
+PAIR = 2 * BLK
+CHUNK = 4 * BLK + 16
+PIECE = 256
+
+
+def contract(a, b, da, db):
+    return lax.dot_general(a, b, (((da,), (db,)), ((), ())), preferred_element_type=jnp.float32)
+
+
+def fused_kernel(
+    n,
+    q_ref,
+    k_ref,
+    v_ref,
+    o_ref,
+    g_ref,
+    map_ref,
+    wq_hbm,
+    wk_hbm,
+    wv_hbm,
+    out_ref,
+    held,
+    bias,
+    dk_acc,
+    dv_acc,
+    grads,
+    w_ref,
+    to_sib,
+    from_sib,
+    to_far,
+    from_far,
+    w_sem,
+    ctx_send,
+    ctx_recv,
+    sib_send,
+    sib_recv,
+    far_send,
+    far_recv,
+):
+    heads = q_ref.shape[1] // HD
+    depth = n // 2
+    tokens = n * BLK
+    pieces = to_far.shape[0]
+    block_rows = to_far.shape[1]
+    c = lax.axis_index("ctx")
+    t = lax.axis_index("tp")
+    z = c // 2
+    other = c + 1 - 2 * (c % 2)
+    sib = t + 1 - 2 * (t % 2)
+    far = (t + 2) % 4
+    scale = 1.0 / math.sqrt(HD)
+
+    barrier = pltpu.get_barrier_semaphore()
+    for peer in ({"ctx": other}, {"tp": sib}, {"tp": far}):
+        pl.semaphore_signal(barrier, inc=1, device_id=peer, device_id_type=MESH)
+
+    @pl.when(z > 0)
+    def _():
+        pl.semaphore_signal(barrier, inc=1, device_id={"ctx": c - 2}, device_id_type=MESH)
+
+    @pl.when(z < depth - 1)
+    def _():
+        pl.semaphore_signal(barrier, inc=1, device_id={"ctx": c + 2}, device_id_type=MESH)
+
+    w_copies = [
+        pltpu.make_async_copy(w, w_ref.at[:, pl.ds(i * heads * HD, heads * HD)], w_sem.at[i])
+        for i, w in enumerate((wq_hbm, wk_hbm, wv_hbm))
+    ]
+    for copy in w_copies:
+        copy.start()
+
+    for h in range(heads):
+        cols = slice(h * HD, (h + 1) * HD)
+        held[h, c, 0:BLK, :] = q_ref[:, cols]
+        held[h, c, BLK : 2 * BLK, :] = k_ref[:, cols]
+        held[h, c, 2 * BLK : 3 * BLK, :] = v_ref[:, cols]
+        held[h, c, 3 * BLK : 4 * BLK, :] = g_ref[:, cols]
+        product = g_ref[:, cols].astype(jnp.float32) * o_ref[:, cols].astype(jnp.float32)
+        delta = jnp.sum(product.T, axis=0, keepdims=True)
+        high = delta.astype(jnp.bfloat16)
+        rest = delta - high.astype(jnp.float32)
+        middle = rest.astype(jnp.bfloat16)
+        low = (rest - middle.astype(jnp.float32)).astype(jnp.bfloat16)
+        held[h, c, 4 * BLK : CHUNK, :] = jnp.concatenate(
+            [high, middle, low, jnp.zeros((CHUNK - 4 * BLK - 3, BLK), jnp.bfloat16)], axis=0
+        )
+
+    def ctx_copy(h, slab, way, target):
+        return pltpu.make_async_remote_copy(
+            src_ref=held.at[h, slab],
+            dst_ref=held.at[h, slab],
+            send_sem=ctx_send.at[h, way, slab],
+            recv_sem=ctx_recv.at[h, slab],
+            device_id={"ctx": target},
+            device_id_type=MESH,
+        )
+
+    def send_up(h, slab):
+        @pl.when(z < depth - 1)
+        def _():
+            ctx_copy(h, slab, 0, c + 2).start()
+
+    def send_down(h, slab):
+        @pl.when(z > 0)
+        def _():
+            ctx_copy(h, slab, 1, c - 2).start()
+
+    def send_own(h):
+        send_up(h, c)
+        send_down(h, c)
+        ctx_copy(h, c, 2, other).start()
+
+    def pass_on(h, d):
+        @pl.when(z - d >= 0)
+        def _():
+            slab = c - 2 * d
+            ctx_copy(h, slab, 0, c).wait_recv()
+            send_up(h, slab)
+            ctx_copy(h, slab, 2, other).start()
+
+        @pl.when(z + d < depth)
+        def _():
+            slab = c + 2 * d
+            ctx_copy(h, slab, 0, c).wait_recv()
+            send_down(h, slab)
+            ctx_copy(h, slab, 2, other).start()
+
+    pl.semaphore_wait(
+        barrier,
+        3 + jnp.where(z > 0, 1, 0) + jnp.where(z < depth - 1, 1, 0),
+    )
+    send_own(0)
+    send_own(1)
+
+    for a in range(n):
+        for b in range(n):
+            bias[b : b + 1, a * BLK : (a + 1) * BLK] = jnp.full(
+                (1, BLK), jnp.where(map_ref[a, b] > 0, 0.0, NEG_FILL), jnp.float32
+            )
+
+    def attend(h, i):
+        first = 2 * i
+        keys = held[h, :, BLK : 2 * BLK, :].reshape(tokens, HD)
+        values = held[h, :, 2 * BLK : 3 * BLK, :].reshape(tokens, HD)
+        pair_q = held[h, pl.ds(first, 2), 0:BLK, :].reshape(PAIR, HD)
+        pair_g = held[h, pl.ds(first, 2), 3 * BLK : 4 * BLK, :].reshape(PAIR, HD)
+        tails = held[h, pl.ds(first, 2), 4 * BLK : CHUNK, :].astype(jnp.float32)
+        sums = jnp.sum(tails, axis=1)
+        delta = jnp.concatenate([sums[0:1], sums[1:2]], axis=1)
+        columns = pl.ds(pl.multiple_of(i * PAIR, PAIR), PAIR)
+        scores = contract(keys, pair_q, 1, 1) * (scale * LOG2E)
+        masked = scores.reshape(n, BLK, PAIR) + bias[:, columns][:, None, :]
+        top = jnp.max(masked, axis=(0, 1), keepdims=True)
+        raised = jnp.exp2(masked - top)
+        total = jnp.sum(raised, axis=(0, 1), keepdims=True)
+        probs = (raised * (1.0 / total)).reshape(tokens, PAIR)
+        dprobs = contract(values, pair_g, 1, 1)
+        dscores = (probs * (dprobs - delta)).astype(jnp.bfloat16)
+        probs_low = probs.astype(jnp.bfloat16)
+        dv_part = contract(probs_low, pair_g, 1, 0)
+        dk_part = contract(dscores, pair_q, 1, 0)
+        dv_acc[...] += dv_part
+        dk_acc[...] += dk_part
+        dq = contract(dscores, keys, 0, 0) * scale
+        grads[pl.ds(pl.multiple_of(i * PAIR, PAIR), PAIR), h * HD : (h + 1) * HD] = dq.astype(
+            jnp.bfloat16
+        )
+
+    def finish_head(h):
+        base = heads * HD
+        grads[:, base + h * HD : base + (h + 1) * HD] = (dk_acc[...] * scale).astype(jnp.bfloat16)
+        grads[:, 2 * base + h * HD : 2 * base + (h + 1) * HD] = dv_acc[...].astype(jnp.bfloat16)
+
+    def clear():
+        dk_acc[...] = jnp.zeros_like(dk_acc)
+        dv_acc[...] = jnp.zeros_like(dv_acc)
+
+    def passive(h):
+        def one(j, carry):
+            ctx_copy(h, (1 - c % 2) + 2 * j, 0, c).wait_recv()
+            return carry
+
+        lax.fori_loop(0, depth, one, 0)
+
+    for d in range(1, depth):
+        pass_on(0, d)
+    passive(0)
+    clear()
+
+    def first_head(i, carry):
+        @pl.when(i >= 1)
+        def _():
+            pass_on(1, i)
+
+        attend(0, i)
+        return carry
+
+    lax.fori_loop(0, n // 2, first_head, 0)
+    finish_head(0)
+    passive(1)
+    clear()
+
+    def second_head(i, carry):
+        attend(1, i)
+        return carry
+
+    lax.fori_loop(0, n // 2, second_head, 0)
+    finish_head(1)
+    for copy in w_copies:
+        copy.wait()
+
+    def term(block, p):
+        rows = grads[pl.ds(pl.multiple_of(block * block_rows, block_rows), block_rows), :]
+        return contract(rows, w_ref[pl.ds(pl.multiple_of(p * PIECE, PIECE), PIECE), :], 1, 1)
+
+    def sib_copy(k, p):
+        return pltpu.make_async_remote_copy(
+            src_ref=to_sib.at[k, p],
+            dst_ref=from_sib.at[k, p],
+            send_sem=sib_send.at[k, p],
+            recv_sem=sib_recv.at[k, p],
+            device_id={"tp": sib},
+            device_id_type=MESH,
+        )
+
+    def far_copy(p):
+        return pltpu.make_async_remote_copy(
+            src_ref=to_far.at[p],
+            dst_ref=from_far.at[p],
+            send_sem=far_send.at[p],
+            recv_sem=far_recv.at[p],
+            device_id={"tp": far},
+            device_id_type=MESH,
+        )
+
+    def for_sib(k, block):
+        def one(p, carry):
+            to_sib[k, p] = term(block, p).astype(jnp.bfloat16)
+            sib_copy(k, p).start()
+            return carry
+
+        lax.fori_loop(0, pieces, one, 0)
+
+    def for_far(p, carry):
+        own = term(far, p)
+        sib_copy(0, p).wait_recv()
+        to_far[p] = (own + from_sib[0, p].astype(jnp.float32)).astype(jnp.bfloat16)
+        far_copy(p).start()
+        return carry
+
+    def for_out(p, carry):
+        own = term(t, p)
+        sib_copy(1, p).wait_recv()
+        own = own + from_sib[1, p].astype(jnp.float32)
+        far_copy(p).wait_recv()
+        out_ref[:, pl.ds(pl.multiple_of(p * PIECE, PIECE), PIECE)] = (
+            own + from_far[p].astype(jnp.float32)
+        ).astype(jnp.bfloat16)
+        return carry
+
+    for_sib(0, (sib + 2) % 4)
+    lax.fori_loop(0, pieces, for_far, 0)
+    for_sib(1, sib)
+    lax.fori_loop(0, pieces, for_out, 0)
+
+    def drain(p, carry):
+        sib_copy(0, p).wait_send()
+        sib_copy(1, p).wait_send()
+        far_copy(p).wait_send()
+        return carry
+
+    lax.fori_loop(0, pieces, drain, 0)
+
+    def drain_ctx(j, carry):
+        slab = c % 2 + 2 * j
+        for h in range(heads):
+            ctx_copy(h, slab, 2, c).wait_send()
+
+            @pl.when((j <= z) & (z < depth - 1))
+            def _():
+                ctx_copy(h, slab, 0, c).wait_send()
+
+            @pl.when((j >= z) & (z > 0))
+            def _():
+                ctx_copy(h, slab, 1, c).wait_send()
+
+        return carry
+
+    lax.fori_loop(0, depth, drain_ctx, 0)
+
+
+def fused_device(
+    n,
+    queries,
+    key_states,
+    value_states,
+    attn_output,
+    output_grad,
+    block_map,
+    w_query,
+    w_key,
+    w_value,
+):
+    slab_rows, width = queries.shape
+    heads = width // HD
+    tokens = n * slab_rows
+    model = w_query.shape[0]
+    block_rows = tokens // 4
+    pieces = model // PIECE
+    vmem = pl.BlockSpec(memory_space=pltpu.VMEM)
+    dma = pltpu.SemaphoreType.DMA
+    return pl.pallas_call(
+        functools.partial(fused_kernel, n),
+        out_shape=jax.ShapeDtypeStruct((block_rows, model), jnp.bfloat16),
+        in_specs=[vmem] * 5
+        + [pl.BlockSpec(memory_space=pltpu.SMEM)]
+        + [pl.BlockSpec(memory_space=pl.ANY)] * 3,
+        out_specs=vmem,
+        scratch_shapes=[
+            pltpu.VMEM((heads, n, CHUNK, HD), jnp.bfloat16),
+            pltpu.VMEM((n, tokens), jnp.float32),
+            pltpu.VMEM((tokens, HD), jnp.float32),
+            pltpu.VMEM((tokens, HD), jnp.float32),
+            pltpu.VMEM((tokens, 3 * width), jnp.bfloat16),
+            pltpu.VMEM((model, 3 * width), jnp.bfloat16),
+            pltpu.VMEM((2, pieces, block_rows, PIECE), jnp.bfloat16),
+            pltpu.VMEM((2, pieces, block_rows, PIECE), jnp.bfloat16),
+            pltpu.VMEM((pieces, block_rows, PIECE), jnp.bfloat16),
+            pltpu.VMEM((pieces, block_rows, PIECE), jnp.bfloat16),
+            dma((3,)),
+            dma((heads, 3, n)),
+            dma((heads, n)),
+            dma((2, pieces)),
+            dma((2, pieces)),
+            dma((pieces,)),
+            dma((pieces,)),
+        ],
+        compiler_params=pltpu.CompilerParams(
+            collective_id=0, has_side_effects=True, vmem_limit_bytes=48 * 1024 * 1024
+        ),
+        cost_estimate=pl.CostEstimate(
+            flops=10 * heads * tokens * tokens * HD + 6 * tokens * model * width,
+            bytes_accessed=6 * model * width + 2 * block_rows * model,
+            transcendentals=heads * tokens * tokens,
+        ),
+    )(
+        queries,
+        key_states,
+        value_states,
+        attn_output,
+        output_grad,
+        block_map,
+        w_query,
+        w_key,
+        w_value,
+    )
+
+
 def solution(mesh):
+    context_count, group_count = mesh.shape["ctx"], mesh.shape["tp"]
+    if context_count == 8 and group_count == 4:
+        body = functools.partial(fused_device, context_count)
+    else:
+        body = per_device
     return jax.shard_map(
-        per_device,
+        body,
         mesh=mesh,
         in_specs=(
             P("ctx", "tp"),

time: 202 us -> 65.5 us (0.32)
  waiting for transfers between devices: 89.4 us -> 0 us
  blocking collectives: 64.5 us -> 0 us
  Pallas kernels: 0 us -> 56.2 us
  between operations: 13.6 us -> 0.02 us
  other arithmetic: 7.33 us -> 0 us
  matrix products: 6.06 us -> 0 us
  starting transfers between devices: 5.83 us -> 0 us
  loops' own time: 5.34 us -> 0 us
    all_gather x2 -> x0, blocking collectives: 64.5 us -> none  [the longest x1 33.2 us: per_device(): lax.all_gather(key_states, 'ctx', axis=0, tiled=True)]
    pallas_call x0 -> x1, Pallas kernels: none -> 56.2 us  [fused_device(): pl.pallas_call(functools.partial(fused_kernel, n), out_shape=jax.ShapeDty...]
    all_gather x1 -> x0, waiting for transfers between devices: 42.9 us -> none  [per_device(): gradients = lax.all_gather(own_grads, 'ctx', axis=0, tiled=True)]
    reduce_scatter x1 -> x0, waiting for transfers between devices: 30.4 us -> none  [per_device(): lax.psum_scatter(lax.dot_general(gradients, projections, (((1,), (1,)), (...]
    all_to_all x1 -> x0, waiting for transfers between devices: 16.1 us -> none  [per_device(): lax.all_to_all(part_grads.reshape(context_count, slab_rows, part_width),...]
    unnamed x10 -> x19, local copies, waits for them, and re-layouts: 1.93 us -> 8.8 us
    dot_general x7 -> x0, matrix products: 6.06 us -> none  [the longest x1 4.58 us: per_device(): lax.dot_general(gradients, projections, (((1,), (1,)), ((), ())), preferr...]
    all_to_all x1 -> x0, starting transfers between devices: 5.75 us -> none  [per_device(): lax.all_to_all(part_grads.reshape(context_count, slab_rows, part_width),...]
  transfers between devices with their start and end apart: 3 -> 0, of which waited for: 3 -> 0; matrix products, arithmetic and copies ran while one was open for 0% -> 0% of each run, Pallas kernels for 0% -> 0%
where the time goes in v1:
time: 65.5 us; the launch traced here: 65 us
  Pallas kernels  56.2 us (86%)
  local copies, waits for them, and re-layouts  8.8 us (13%)
    pallas_call x1, Pallas kernels, fused_device(): pl.pallas_call(functools.partial(fused_kernel, n), out_shape=jax.ShapeDty...  56.2 us
    unnamed x19, local copies, waits for them, and re-layouts  8.8 us

profile of v1, /device:TPU:0, one launch (start us, length us, event | category | flops | bytes accessed | tf_op | source)
XLA Modules:
  0.0 65.0 jit_solution(6040780880417556375)
XLA Ops:
  0.0 0.0 copy-start
  0.0 1.0 %copy-done = bf16[1024,256]{1,0:T(8,128)(2,1)S(1)} copy-done((bf16[1024,256]{1,0:T(8,128)(2,1)S(1)}, bf16[1024,256]{1,0:T(8,128)(2,1)}, u32[]{:S(2)}) %copy-start) | copy-done | bytes 524312
  1.0 0.0 copy-start.1
  1.0 1.0 %copy-done.1 = bf16[1024,256]{1,0:T(8,128)(2,1)S(1)} copy-done((bf16[1024,256]{1,0:T(8,128)(2,1)S(1)}, bf16[1024,256]{1,0:T(8,128)(2,1)}, u32[]{:S(2)}) %copy-start.1) | copy-done | bytes 524312
  2.1 0.0 copy-start.2
  2.1 1.0 %copy-done.2 = bf16[1024,256]{1,0:T(8,128)(2,1)S(1)} copy-done((bf16[1024,256]{1,0:T(8,128)(2,1)S(1)}, bf16[1024,256]{1,0:T(8,128)(2,1)}, u32[]{:S(2)}) %copy-start.2) | copy-done | bytes 524312
  3.1 0.0 copy-start.3
  3.1 0.8 %copy-done.3 = bf16[128,256]{1,0:T(8,128)(2,1)S(1)} copy-done((bf16[128,256]{1,0:T(8,128)(2,1)S(1)}, bf16[128,256]{1,0:T(8,128)(2,1)}, u32[]{:S(2)}) %copy-start.3) | copy-done | bytes 65560
  4.0 0.0 copy-start.4
  4.0 0.8 %copy-done.4 = bf16[128,256]{1,0:T(8,128)(2,1)S(1)} copy-done((bf16[128,256]{1,0:T(8,128)(2,1)S(1)}, bf16[128,256]{1,0:T(8,128)(2,1)}, u32[]{:S(2)}) %copy-start.4) | copy-done | bytes 65560
  4.8 0.0 copy-start.5
  4.8 0.8 %copy-done.5 = bf16[128,256]{1,0:T(8,128)(2,1)S(1)} copy-done((bf16[128,256]{1,0:T(8,128)(2,1)S(1)}, bf16[128,256]{1,0:T(8,128)(2,1)}, u32[]{:S(2)}) %copy-start.5) | copy-done | bytes 65560
  5.6 0.0 copy-start.6
  5.6 0.8 %copy-done.6 = bf16[128,256]{1,0:T(8,128)(2,1)S(1)} copy-done((bf16[128,256]{1,0:T(8,128)(2,1)S(1)}, bf16[128,256]{1,0:T(8,128)(2,1)}, u32[]{:S(2)}) %copy-start.6) | copy-done | bytes 65560
  6.5 0.0 copy-start.7
  6.5 0.8 %copy-done.7 = bf16[128,256]{1,0:T(8,128)(2,1)S(1)} copy-done((bf16[128,256]{1,0:T(8,128)(2,1)S(1)}, bf16[128,256]{1,0:T(8,128)(2,1)}, u32[]{:S(2)}) %copy-start.7) | copy-done | bytes 65560
  7.3 0.0 copy-start.8
  7.3 0.7 %copy-done.8 = s32[8,8]{1,0:T(8,128)S(1)} copy-done((s32[8,8]{1,0:T(8,128)S(1)}, s32[8,8]{1,0:T(8,128)}, u32[]{:S(2)}) %copy-start.8) | copy-done | bytes 280
  8.0 56.2 %shard_map.91 = bf16[256,1024]{1,0:T(8,128)(2,1)S(1)} custom-call(bf16[128,256]{1,0:T(8,128)(2,1)S(1)} %copy-done.3, bf16[128,256]{1,0:T(8,128)(2,1)S(1)} %copy-done.4, bf16[128,256]{1,0:T(8,128)(2,1)S(1)} %copy-done.5, bf16[128,256]{1,0:T(8,128)(2,1)S(1)} %copy-done.6, bf16[128,256]{1,0:T(8,128)(2,1)S(1)} %copy-done.7, s32[8,8]{1,0:T(8,128)S(1)} %copy-done.8, ...), custom_call_target="tpu_custom_call" | custom-call | flops 4294967296 | bytes 2097152 | tf_op jit(solution)/shard_map/pallas_call | solution.py:480
  64.2 0.8 %copy.11 = bf16[256,1024]{1,0:T(8,128)(2,1)} copy(bf16[256,1024]{1,0:T(8,128)(2,1)S(1)} %shard_map.91) | data formatting | bytes 1048576
Async XLA Ops:
  0.0 1.0 %copy-start = (bf16[1024,256]{1,0:T(8,128)(2,1)S(1)}, bf16[1024,256]{1,0:T(8,128)(2,1)}, u32[]{:S(2)}) copy-start(bf16[1024,256]{1,0:T(8,128)(2,1)} %wq_hbm.1) | copy-start | bytes 1572868
  1.0 1.0 %copy-start.1 = (bf16[1024,256]{1,0:T(8,128)(2,1)S(1)}, bf16[1024,256]{1,0:T(8,128)(2,1)}, u32[]{:S(2)}) copy-start(bf16[1024,256]{1,0:T(8,128)(2,1)} %wk_hbm.1) | copy-start | bytes 1572868
  2.1 1.0 %copy-start.2 = (bf16[1024,256]{1,0:T(8,128)(2,1)S(1)}, bf16[1024,256]{1,0:T(8,128)(2,1)}, u32[]{:S(2)}) copy-start(bf16[1024,256]{1,0:T(8,128)(2,1)} %wv_hbm.1) | copy-start | bytes 1572868
  3.1 0.8 %copy-start.3 = (bf16[128,256]{1,0:T(8,128)(2,1)S(1)}, bf16[128,256]{1,0:T(8,128)(2,1)}, u32[]{:S(2)}) copy-start(bf16[128,256]{1,0:T(8,128)(2,1)} %q_ref.1) | copy-start | bytes 196612
  4.0 0.8 %copy-start.4 = (bf16[128,256]{1,0:T(8,128)(2,1)S(1)}, bf16[128,256]{1,0:T(8,128)(2,1)}, u32[]{:S(2)}) copy-start(bf16[128,256]{1,0:T(8,128)(2,1)} %k_ref.1) | copy-start | bytes 196612
  4.8 0.8 %copy-start.5 = (bf16[128,256]{1,0:T(8,128)(2,1)S(1)}, bf16[128,256]{1,0:T(8,128)(2,1)}, u32[]{:S(2)}) copy-start(bf16[128,256]{1,0:T(8,128)(2,1)} %v_ref.1) | copy-start | bytes 196612
  5.6 0.8 %copy-start.6 = (bf16[128,256]{1,0:T(8,128)(2,1)S(1)}, bf16[128,256]{1,0:T(8,128)(2,1)}, u32[]{:S(2)}) copy-start(bf16[128,256]{1,0:T(8,128)(2,1)} %o_ref.1) | copy-start | bytes 196612
  6.5 0.8 %copy-start.7 = (bf16[128,256]{1,0:T(8,128)(2,1)S(1)}, bf16[128,256]{1,0:T(8,128)(2,1)}, u32[]{:S(2)}) copy-start(bf16[128,256]{1,0:T(8,128)(2,1)} %g_ref.1) | copy-start | bytes 196612
  7.3 0.7 %copy-start.8 = (s32[8,8]{1,0:T(8,128)S(1)}, s32[8,8]{1,0:T(8,128)}, u32[]{:S(2)}) copy-start(s32[8,8]{1,0:T(8,128)} %map_ref.1) | copy-start | bytes 772

commit v2 on v1

--- a/solution.py
+++ b/solution.py
@@ -167,7 +167,7 @@
 MESH = pl.DeviceIdType.MESH
 LOG2E = 1.4426950408889634
 PAIR = 2 * BLK
-CHUNK = 4 * BLK + 16
+TAIL = 16
 PIECE = 256
 
 
@@ -177,20 +177,24 @@
 
 def fused_kernel(
     n,
-    q_ref,
-    k_ref,
-    v_ref,
-    o_ref,
-    g_ref,
+    q_hbm,
+    k_hbm,
+    v_hbm,
+    o_hbm,
+    g_hbm,
     map_ref,
     wq_hbm,
     wk_hbm,
     wv_hbm,
     out_ref,
-    held,
+    held_qk,
+    held_g,
+    held_v,
+    o_ref,
     bias,
-    dk_acc,
-    dv_acc,
+    probs_ref,
+    delta_ref,
+    dq_acc,
     grads,
     w_ref,
     to_sib,
@@ -198,6 +202,7 @@
     to_far,
     from_far,
     w_sem,
+    in_sem,
     ctx_send,
     ctx_recv,
     sib_send,
@@ -205,7 +210,7 @@
     far_send,
     far_recv,
 ):
-    heads = q_ref.shape[1] // HD
+    heads = held_qk.shape[0]
     depth = n // 2
     tokens = n * BLK
     pieces = to_far.shape[0]
@@ -230,35 +235,53 @@
     def _():
         pl.semaphore_signal(barrier, inc=1, device_id={"ctx": c + 2}, device_id_type=MESH)
 
+    in_copies = [pltpu.make_async_copy(o_hbm, o_ref, in_sem.at[4 * heads])]
+    for h in range(heads):
+        cols = pl.ds(h * HD, HD)
+        for i, (source, target) in enumerate(
+            (
+                (q_hbm, held_qk.at[h, c, pl.ds(0, BLK)]),
+                (k_hbm, held_qk.at[h, c, pl.ds(BLK, BLK)]),
+                (g_hbm, held_g.at[h, c, pl.ds(0, BLK)]),
+                (v_hbm, held_v.at[h, c]),
+            )
+        ):
+            in_copies.append(
+                pltpu.make_async_copy(source.at[:, cols], target, in_sem.at[4 * h + i])
+            )
+    for copy in in_copies:
+        copy.start()
     w_copies = [
         pltpu.make_async_copy(w, w_ref.at[:, pl.ds(i * heads * HD, heads * HD)], w_sem.at[i])
         for i, w in enumerate((wq_hbm, wk_hbm, wv_hbm))
     ]
     for copy in w_copies:
         copy.start()
+    for copy in in_copies:
+        copy.wait()
 
     for h in range(heads):
-        cols = slice(h * HD, (h + 1) * HD)
-        held[h, c, 0:BLK, :] = q_ref[:, cols]
-        held[h, c, BLK : 2 * BLK, :] = k_ref[:, cols]
-        held[h, c, 2 * BLK : 3 * BLK, :] = v_ref[:, cols]
-        held[h, c, 3 * BLK : 4 * BLK, :] = g_ref[:, cols]
-        product = g_ref[:, cols].astype(jnp.float32) * o_ref[:, cols].astype(jnp.float32)
+        grad = held_g[h, c, 0:BLK, :].astype(jnp.float32)
+        product = grad * o_ref[:, h * HD : (h + 1) * HD].astype(jnp.float32)
         delta = jnp.sum(product.T, axis=0, keepdims=True)
         high = delta.astype(jnp.bfloat16)
         rest = delta - high.astype(jnp.float32)
         middle = rest.astype(jnp.bfloat16)
         low = (rest - middle.astype(jnp.float32)).astype(jnp.bfloat16)
-        held[h, c, 4 * BLK : CHUNK, :] = jnp.concatenate(
-            [high, middle, low, jnp.zeros((CHUNK - 4 * BLK - 3, BLK), jnp.bfloat16)], axis=0
-        )
-
-    def ctx_copy(h, slab, way, target):
+        held_g[h, c, BLK : BLK + TAIL, :] = jnp.concatenate(
+            [high, middle, low, jnp.zeros((TAIL - 3, BLK), jnp.bfloat16)], axis=0
+        )
+
+    stores = (held_qk, held_g, held_v)
+    streams = [(kind, h) for kind in range(3) for h in range(heads)]
+
+    def ctx_copy(s, slab, way, target):
+        kind, h = streams[s]
         return pltpu.make_async_remote_copy(
-            src_ref=held.at[h, slab],
-            dst_ref=held.at[h, slab],
-            send_sem=ctx_send.at[h, way, slab],
-            recv_sem=ctx_recv.at[h, slab],
+            src_ref=stores[kind].at[h, slab],
+            dst_ref=stores[kind].at[h, slab],
+            send_sem=ctx_send.at[s, way, slab],
+            recv_sem=ctx_recv.at[s, slab],
             device_id={"ctx": target},
             device_id_type=MESH,
         )
@@ -305,16 +328,11 @@
             bias[b : b + 1, a * BLK : (a + 1) * BLK] = jnp.full(
                 (1, BLK), jnp.where(map_ref[a, b] > 0, 0.0, NEG_FILL), jnp.float32
             )
-
-    def attend(h, i):
-        first = 2 * i
-        keys = held[h, :, BLK : 2 * BLK, :].reshape(tokens, HD)
-        values = held[h, :, 2 * BLK : 3 * BLK, :].reshape(tokens, HD)
-        pair_q = held[h, pl.ds(first, 2), 0:BLK, :].reshape(PAIR, HD)
-        pair_g = held[h, pl.ds(first, 2), 3 * BLK : 4 * BLK, :].reshape(PAIR, HD)
-        tails = held[h, pl.ds(first, 2), 4 * BLK : CHUNK, :].astype(jnp.float32)
-        sums = jnp.sum(tails, axis=1)
-        delta = jnp.concatenate([sums[0:1], sums[1:2]], axis=1)
+    dq_acc[...] = jnp.zeros_like(dq_acc)
+
+    def soften(h, i):
+        keys = held_qk[h, :, BLK : 2 * BLK, :].reshape(tokens, HD)
+        pair_q = held_qk[h, pl.ds(2 * i, 2), 0:BLK, :].reshape(PAIR, HD)
         columns = pl.ds(pl.multiple_of(i * PAIR, PAIR), PAIR)
         scores = contract(keys, pair_q, 1, 1) * (scale * LOG2E)
         masked = scores.reshape(n, BLK, PAIR) + bias[:, columns][:, None, :]
@@ -322,58 +340,68 @@
         raised = jnp.exp2(masked - top)
         total = jnp.sum(raised, axis=(0, 1), keepdims=True)
         probs = (raised * (1.0 / total)).reshape(tokens, PAIR)
-        dprobs = contract(values, pair_g, 1, 1)
-        dscores = (probs * (dprobs - delta)).astype(jnp.bfloat16)
-        probs_low = probs.astype(jnp.bfloat16)
-        dv_part = contract(probs_low, pair_g, 1, 0)
-        dk_part = contract(dscores, pair_q, 1, 0)
-        dv_acc[...] += dv_part
-        dk_acc[...] += dk_part
-        dq = contract(dscores, keys, 0, 0) * scale
-        grads[pl.ds(pl.multiple_of(i * PAIR, PAIR), PAIR), h * HD : (h + 1) * HD] = dq.astype(
+        probs_ref[h, :, columns] = probs.astype(jnp.bfloat16)
+
+    def value_rows(h, i):
+        rows = pl.ds(pl.multiple_of(i * PAIR, PAIR), PAIR)
+        all_g = held_g[h, :, 0:BLK, :].reshape(tokens, HD)
+        first = (2 * heads + h) * HD
+        grads[rows, first : first + HD] = contract(probs_ref[h, rows, :], all_g, 1, 0).astype(
             jnp.bfloat16
         )
 
-    def finish_head(h):
-        base = heads * HD
-        grads[:, base + h * HD : base + (h + 1) * HD] = (dk_acc[...] * scale).astype(jnp.bfloat16)
-        grads[:, 2 * base + h * HD : 2 * base + (h + 1) * HD] = dv_acc[...].astype(jnp.bfloat16)
-
-    def clear():
-        dk_acc[...] = jnp.zeros_like(dk_acc)
-        dv_acc[...] = jnp.zeros_like(dv_acc)
-
-    def passive(h):
+    def key_rows(h, i):
+        rows = pl.ds(pl.multiple_of(i * PAIR, PAIR), PAIR)
+        pair = pl.ds(2 * i, 2)
+        all_g = held_g[h, :, 0:BLK, :].reshape(tokens, HD)
+        all_q = held_qk[h, :, 0:BLK, :].reshape(tokens, HD)
+        keys = held_qk[h, pair, BLK : 2 * BLK, :].reshape(PAIR, HD)
+        values = held_v[h, pair, :, :].reshape(PAIR, HD)
+        dprobs = contract(values, all_g, 1, 1)
+        probs = probs_ref[h, rows, :].astype(jnp.float32)
+        dscores = (probs * (dprobs - delta_ref[h : h + 1, :])).astype(jnp.bfloat16)
+        first = (heads + h) * HD
+        grads[rows, first : first + HD] = (contract(dscores, all_q, 1, 0) * scale).astype(
+            jnp.bfloat16
+        )
+        dq_acc[h] += contract(keys, dscores, 0, 0)
+
+    def spread_delta(h):
+        sums = jnp.sum(held_g[h, :, BLK : BLK + TAIL, :].astype(jnp.float32), axis=1)
+        for a in range(n):
+            delta_ref[h : h + 1, a * BLK : (a + 1) * BLK] = sums[a : a + 1]
+
+    def passive(s):
         def one(j, carry):
-            ctx_copy(h, (1 - c % 2) + 2 * j, 0, c).wait_recv()
+            ctx_copy(s, (1 - c % 2) + 2 * j, 0, c).wait_recv()
             return carry
 
         lax.fori_loop(0, depth, one, 0)
 
+    last = len(streams) - 1
     for d in range(1, depth):
         pass_on(0, d)
-    passive(0)
-    clear()
-
-    def first_head(i, carry):
-        @pl.when(i >= 1)
-        def _():
-            pass_on(1, i)
-
-        attend(0, i)
-        return carry
-
-    lax.fori_loop(0, n // 2, first_head, 0)
-    finish_head(0)
-    passive(1)
-    clear()
-
-    def second_head(i, carry):
-        attend(1, i)
-        return carry
-
-    lax.fori_loop(0, n // 2, second_head, 0)
-    finish_head(1)
+    for s, (kind, h) in enumerate(streams):
+        passive(s)
+        if s + 2 <= last:
+            send_own(s + 2)
+        if kind == 1:
+            spread_delta(h)
+        work = (soften, value_rows, key_rows)[kind]
+
+        def step(i, carry, s=s, h=h, work=work):
+            if s < last:
+
+                @pl.when(i >= 1)
+                def _():
+                    pass_on(s + 1, i)
+
+            work(h, i)
+            return carry
+
+        lax.fori_loop(0, depth, step, 0)
+        if kind == 2:
+            grads[:, h * HD : (h + 1) * HD] = (dq_acc[h].T * scale).astype(jnp.bfloat16)
     for copy in w_copies:
         copy.wait()
 
@@ -441,7 +469,7 @@
 
     def drain_ctx(j, carry):
         slab = c % 2 + 2 * j
-        for h in range(heads):
+        for h in range(len(streams)):
             ctx_copy(h, slab, 2, c).wait_send()
 
             @pl.when((j <= z) & (z < depth - 1))
@@ -480,15 +508,19 @@
     return pl.pallas_call(
         functools.partial(fused_kernel, n),
         out_shape=jax.ShapeDtypeStruct((block_rows, model), jnp.bfloat16),
-        in_specs=[vmem] * 5
+        in_specs=[pl.BlockSpec(memory_space=pl.ANY)] * 5
         + [pl.BlockSpec(memory_space=pltpu.SMEM)]
         + [pl.BlockSpec(memory_space=pl.ANY)] * 3,
         out_specs=vmem,
         scratch_shapes=[
-            pltpu.VMEM((heads, n, CHUNK, HD), jnp.bfloat16),
+            pltpu.VMEM((heads, n, 2 * BLK, HD), jnp.bfloat16),
+            pltpu.VMEM((heads, n, BLK + TAIL, HD), jnp.bfloat16),
+            pltpu.VMEM((heads, n, BLK, HD), jnp.bfloat16),
+            pltpu.VMEM((slab_rows, width), jnp.bfloat16),
             pltpu.VMEM((n, tokens), jnp.float32),
-            pltpu.VMEM((tokens, HD), jnp.float32),
-            pltpu.VMEM((tokens, HD), jnp.float32),
+            pltpu.VMEM((heads, tokens, tokens), jnp.bfloat16),
+            pltpu.VMEM((heads, tokens), jnp.float32),
+            pltpu.VMEM((heads, HD, tokens), jnp.float32),
             pltpu.VMEM((tokens, 3 * width), jnp.bfloat16),
             pltpu.VMEM((model, 3 * width), jnp.bfloat16),
             pltpu.VMEM((2, pieces, block_rows, PIECE), jnp.bfloat16),
@@ -496,15 +528,16 @@
             pltpu.VMEM((pieces, block_rows, PIECE), jnp.bfloat16),
             pltpu.VMEM((pieces, block_rows, PIECE), jnp.bfloat16),
             dma((3,)),
-            dma((heads, 3, n)),
-            dma((heads, n)),
+            dma((4 * heads + 1,)),
+            dma((3 * heads, 3, n)),
+            dma((3 * heads, n)),
             dma((2, pieces)),
             dma((2, pieces)),
             dma((pieces,)),
             dma((pieces,)),
         ],
         compiler_params=pltpu.CompilerParams(
-            collective_id=0, has_side_effects=True, vmem_limit_bytes=48 * 1024 * 1024
+            collective_id=0, has_side_effects=True, vmem_limit_bytes=62 * 1024 * 1024
         ),
         cost_estimate=pl.CostEstimate(
             flops=10 * heads * tokens * tokens * HD + 6 * tokens * model * width,

time: 65.5 us -> 75 us (1.15)
  Pallas kernels: 56.2 us -> 72.9 us
  local copies, waits for them, and re-layouts: 8.8 us -> 1.87 us
    pallas_call x1, Pallas kernels: 56.2 us -> 72.9 us  [fused_device(): pl.pallas_call(functools.partial(fused_kernel, n), out_shape=jax.ShapeDty...]
    unnamed x19 -> x1, local copies, waits for them, and re-layouts: 8.8 us -> 1.87 us
where the time goes in v2:
time: 75 us; the launch traced here: 74.8 us
  Pallas kernels  72.9 us (97%)
  local copies, waits for them, and re-layouts  1.87 us (2%)
    pallas_call x1, Pallas kernels, fused_device(): pl.pallas_call(functools.partial(fused_kernel, n), out_shape=jax.ShapeDty...  72.9 us
    unnamed x1, local copies, waits for them, and re-layouts  1.87 us

profile of v2, /device:TPU:0, one launch (start us, length us, event | category | flops | bytes accessed | tf_op | source)
XLA Modules:
  0.0 74.8 jit_solution(12242907699189858840)
XLA Ops:
  0.0 72.9 %shard_map.91 = bf16[256,1024]{1,0:T(8,128)(2,1)} custom-call(bf16[128,256]{1,0:T(8,128)(2,1)} %q_hbm.1, bf16[128,256]{1,0:T(8,128)(2,1)} %k_hbm.1, bf16[128,256]{1,0:T(8,128)(2,1)} %v_hbm.1, bf16[128,256]{1,0:T(8,128)(2,1)} %o_hbm.1, bf16[128,256]{1,0:T(8,128)(2,1)} %g_hbm.1, s32[8,8]{1,0:T(8,128)} %map_ref.1, bf16[1024,256]{1,0:T(8,128)(2,1)} %wq_hbm.1, ...), custom_call_target="tpu_custom_call" | custom-call | flops 4294967296 | bytes 2097152 | tf_op jit(solution)/shard_map/pallas_call | solution.py:508
  72.9 1.9 %copy.11 = bf16[256,1024]{1,0:T(8,128)(2,1)} copy(bf16[256,1024]{1,0:T(8,128)(2,1)} %shard_map.91) | data formatting | bytes 1048576

commit v3 on v2

--- a/solution.py
+++ b/solution.py
@@ -189,7 +189,6 @@
     out_ref,
     held_qk,
     held_g,
-    held_v,
     o_ref,
     bias,
     probs_ref,
@@ -243,7 +242,7 @@
                 (q_hbm, held_qk.at[h, c, pl.ds(0, BLK)]),
                 (k_hbm, held_qk.at[h, c, pl.ds(BLK, BLK)]),
                 (g_hbm, held_g.at[h, c, pl.ds(0, BLK)]),
-                (v_hbm, held_v.at[h, c]),
+                (v_hbm, held_g.at[h, c, pl.ds(BLK, BLK)]),
             )
         ):
             in_copies.append(
@@ -268,12 +267,12 @@
         rest = delta - high.astype(jnp.float32)
         middle = rest.astype(jnp.bfloat16)
         low = (rest - middle.astype(jnp.float32)).astype(jnp.bfloat16)
-        held_g[h, c, BLK : BLK + TAIL, :] = jnp.concatenate(
+        held_g[h, c, 2 * BLK : 2 * BLK + TAIL, :] = jnp.concatenate(
             [high, middle, low, jnp.zeros((TAIL - 3, BLK), jnp.bfloat16)], axis=0
         )
 
-    stores = (held_qk, held_g, held_v)
-    streams = [(kind, h) for kind in range(3) for h in range(heads)]
+    stores = (held_qk, held_g)
+    streams = [(kind, h) for kind in range(2) for h in range(heads)]
 
     def ctx_copy(s, slab, way, target):
         kind, h = streams[s]
@@ -320,8 +319,8 @@
         barrier,
         3 + jnp.where(z > 0, 1, 0) + jnp.where(z < depth - 1, 1, 0),
     )
-    send_own(0)
-    send_own(1)
+    for s in range(2):
+        send_own(s)
 
     for a in range(n):
         for b in range(n):
@@ -356,7 +355,7 @@
         all_g = held_g[h, :, 0:BLK, :].reshape(tokens, HD)
         all_q = held_qk[h, :, 0:BLK, :].reshape(tokens, HD)
         keys = held_qk[h, pair, BLK : 2 * BLK, :].reshape(PAIR, HD)
-        values = held_v[h, pair, :, :].reshape(PAIR, HD)
+        values = held_g[h, pair, BLK : 2 * BLK, :].reshape(PAIR, HD)
         dprobs = contract(values, all_g, 1, 1)
         probs = probs_ref[h, rows, :].astype(jnp.float32)
         dscores = (probs * (dprobs - delta_ref[h : h + 1, :])).astype(jnp.bfloat16)
@@ -367,7 +366,7 @@
         dq_acc[h] += contract(keys, dscores, 0, 0)
 
     def spread_delta(h):
-        sums = jnp.sum(held_g[h, :, BLK : BLK + TAIL, :].astype(jnp.float32), axis=1)
+        sums = jnp.sum(held_g[h, :, 2 * BLK : 2 * BLK + TAIL, :].astype(jnp.float32), axis=1)
         for a in range(n):
             delta_ref[h : h + 1, a * BLK : (a + 1) * BLK] = sums[a : a + 1]
 
@@ -378,29 +377,32 @@
 
         lax.fori_loop(0, depth, one, 0)
 
-    last = len(streams) - 1
-    for d in range(1, depth):
-        pass_on(0, d)
-    for s, (kind, h) in enumerate(streams):
+    def backward(h, i):
+        value_rows(h, i)
+        key_rows(h, i)
+
+    count = len(streams)
+    for wave in range(1, count + depth):
+        for d in range(depth - 1, 0, -1):
+            if 0 <= wave - d < count:
+                pass_on(wave - d, d)
+        if wave + 1 < count:
+            send_own(wave + 1)
+        if wave < depth:
+            continue
+        s = wave - depth
+        kind, h = streams[s]
         passive(s)
-        if s + 2 <= last:
-            send_own(s + 2)
         if kind == 1:
             spread_delta(h)
-        work = (soften, value_rows, key_rows)[kind]
-
-        def step(i, carry, s=s, h=h, work=work):
-            if s < last:
-
-                @pl.when(i >= 1)
-                def _():
-                    pass_on(s + 1, i)
-
+        work = (soften, backward)[kind]
+
+        def step(i, carry, h=h, work=work):
             work(h, i)
             return carry
 
         lax.fori_loop(0, depth, step, 0)
-        if kind == 2:
+        if kind == 1:
             grads[:, h * HD : (h + 1) * HD] = (dq_acc[h].T * scale).astype(jnp.bfloat16)
     for copy in w_copies:
         copy.wait()
@@ -514,8 +516,7 @@
         out_specs=vmem,
         scratch_shapes=[
             pltpu.VMEM((heads, n, 2 * BLK, HD), jnp.bfloat16),
-            pltpu.VMEM((heads, n, BLK + TAIL, HD), jnp.bfloat16),
-            pltpu.VMEM((heads, n, BLK, HD), jnp.bfloat16),
+            pltpu.VMEM((heads, n, 2 * BLK + TAIL, HD), jnp.bfloat16),
             pltpu.VMEM((slab_rows, width), jnp.bfloat16),
             pltpu.VMEM((n, tokens), jnp.float32),
             pltpu.VMEM((heads, tokens, tokens), jnp.bfloat16),
@@ -529,8 +530,8 @@
             pltpu.VMEM((pieces, block_rows, PIECE), jnp.bfloat16),
             dma((3,)),
             dma((4 * heads + 1,)),
-            dma((3 * heads, 3, n)),
-            dma((3 * heads, n)),
+            dma((2 * heads, 3, n)),
+            dma((2 * heads, n)),
             dma((2, pieces)),
             dma((2, pieces)),
             dma((pieces,)),

time: 75 us -> 54.1 us (0.72)
  Pallas kernels: 72.9 us -> 52 us
    pallas_call x1, Pallas kernels: 72.9 us -> 52 us  [fused_device(): pl.pallas_call(functools.partial(fused_kernel, n), out_shape=jax.ShapeDty...]
where the time goes in v3:
time: 54.1 us; the launch traced here: 53.9 us
  Pallas kernels  52 us (96%)
  local copies, waits for them, and re-layouts  1.87 us (3%)
    pallas_call x1, Pallas kernels, fused_device(): pl.pallas_call(functools.partial(fused_kernel, n), out_shape=jax.ShapeDty...  52 us
    unnamed x1, local copies, waits for them, and re-layouts  1.87 us

profile of v3, /device:TPU:0, one launch (start us, length us, event | category | flops | bytes accessed | tf_op | source)
XLA Modules:
  0.0 53.9 jit_solution(1731550330647935402)
XLA Ops:
  0.0 52.0 %shard_map.91 = bf16[256,1024]{1,0:T(8,128)(2,1)} custom-call(bf16[128,256]{1,0:T(8,128)(2,1)} %q_hbm.1, bf16[128,256]{1,0:T(8,128)(2,1)} %k_hbm.1, bf16[128,256]{1,0:T(8,128)(2,1)} %v_hbm.1, bf16[128,256]{1,0:T(8,128)(2,1)} %o_hbm.1, bf16[128,256]{1,0:T(8,128)(2,1)} %g_hbm.1, s32[8,8]{1,0:T(8,128)} %map_ref.1, bf16[1024,256]{1,0:T(8,128)(2,1)} %wq_hbm.1, ...), custom_call_target="tpu_custom_call" | custom-call | flops 4294967296 | bytes 2097152 | tf_op jit(solution)/shard_map/pallas_call | solution.py:510
  52.0 1.9 %copy.11 = bf16[256,1024]{1,0:T(8,128)(2,1)} copy(bf16[256,1024]{1,0:T(8,128)(2,1)} %shard_map.91) | data formatting | bytes 1048576

commit v4 on v3

--- a/solution.py
+++ b/solution.py
@@ -220,6 +220,7 @@
     other = c + 1 - 2 * (c % 2)
     sib = t + 1 - 2 * (t % 2)
     far = (t + 2) % 4
+    mate = z + 1 - 2 * (z % 2)
     scale = 1.0 / math.sqrt(HD)
 
     barrier = pltpu.get_barrier_semaphore()
@@ -259,6 +260,81 @@
     for copy in in_copies:
         copy.wait()
 
+    stores = (held_qk, held_g)
+    streams = [(kind, h) for kind in range(2) for h in range(heads)]
+
+    def ctx_copy(s, slab, way, target):
+        kind, h = streams[s]
+        return pltpu.make_async_remote_copy(
+            src_ref=stores[kind].at[h, slab],
+            dst_ref=stores[kind].at[h, slab],
+            send_sem=ctx_send.at[s, way, slab],
+            recv_sem=ctx_recv.at[s, slab],
+            device_id={"ctx": target},
+            device_id_type=MESH,
+        )
+
+    def send_up(h, slab):
+        @pl.when(z < depth - 1)
+        def _():
+            ctx_copy(h, slab, 0, c + 2).start()
+
+    def send_down(h, slab):
+        @pl.when(z > 0)
+        def _():
+            ctx_copy(h, slab, 1, c - 2).start()
+
+    def send_own(h):
+        send_up(h, c)
+        send_down(h, c)
+        ctx_copy(h, c, 2, other).start()
+
+    def relayed(s):
+        return streams[s][0] == 1
+
+    def cross(s, slab):
+        if relayed(s):
+
+            @pl.when(slab // 2 != mate)
+            def _():
+                ctx_copy(s, slab, 2, other).start()
+
+        else:
+            ctx_copy(s, slab, 2, other).start()
+
+    def relay(s):
+        ctx_copy(s, other, 0, c).wait_recv()
+
+        @pl.when(z % 2 == 0)
+        def _():
+            ctx_copy(s, other, 0, c + 2).start()
+
+        @pl.when(z % 2 == 1)
+        def _():
+            ctx_copy(s, other, 1, c - 2).start()
+
+    def pass_on(h, d):
+        @pl.when(z - d >= 0)
+        def _():
+            slab = c - 2 * d
+            ctx_copy(h, slab, 0, c).wait_recv()
+            send_up(h, slab)
+            cross(h, slab)
+
+        @pl.when(z + d < depth)
+        def _():
+            slab = c + 2 * d
+            ctx_copy(h, slab, 0, c).wait_recv()
+            send_down(h, slab)
+            cross(h, slab)
+
+    pl.semaphore_wait(
+        barrier,
+        3 + jnp.where(z > 0, 1, 0) + jnp.where(z < depth - 1, 1, 0),
+    )
+    for s in range(2):
+        send_own(s)
+
     for h in range(heads):
         grad = held_g[h, c, 0:BLK, :].astype(jnp.float32)
         product = grad * o_ref[:, h * HD : (h + 1) * HD].astype(jnp.float32)
@@ -270,57 +346,6 @@
         held_g[h, c, 2 * BLK : 2 * BLK + TAIL, :] = jnp.concatenate(
             [high, middle, low, jnp.zeros((TAIL - 3, BLK), jnp.bfloat16)], axis=0
         )
-
-    stores = (held_qk, held_g)
-    streams = [(kind, h) for kind in range(2) for h in range(heads)]
-
-    def ctx_copy(s, slab, way, target):
-        kind, h = streams[s]
-        return pltpu.make_async_remote_copy(
-            src_ref=stores[kind].at[h, slab],
-            dst_ref=stores[kind].at[h, slab],
-            send_sem=ctx_send.at[s, way, slab],
-            recv_sem=ctx_recv.at[s, slab],
-            device_id={"ctx": target},
-            device_id_type=MESH,
-        )
-
-    def send_up(h, slab):
-        @pl.when(z < depth - 1)
-        def _():
-            ctx_copy(h, slab, 0, c + 2).start()
-
-    def send_down(h, slab):
-        @pl.when(z > 0)
-        def _():
-            ctx_copy(h, slab, 1, c - 2).start()
-
-    def send_own(h):
-        send_up(h, c)
-        send_down(h, c)
-        ctx_copy(h, c, 2, other).start()
-
-    def pass_on(h, d):
-        @pl.when(z - d >= 0)
-        def _():
-            slab = c - 2 * d
-            ctx_copy(h, slab, 0, c).wait_recv()
-            send_up(h, slab)
-            ctx_copy(h, slab, 2, other).start()
-
-        @pl.when(z + d < depth)
-        def _():
-            slab = c + 2 * d
-            ctx_copy(h, slab, 0, c).wait_recv()
-            send_down(h, slab)
-            ctx_copy(h, slab, 2, other).start()
-
-    pl.semaphore_wait(
-        barrier,
-        3 + jnp.where(z > 0, 1, 0) + jnp.where(z < depth - 1, 1, 0),
-    )
-    for s in range(2):
-        send_own(s)
 
     for a in range(n):
         for b in range(n):
@@ -372,7 +397,13 @@
 
     def passive(s):
         def one(j, carry):
-            ctx_copy(s, (1 - c % 2) + 2 * j, 0, c).wait_recv()
+            def arrive():
+                ctx_copy(s, (1 - c % 2) + 2 * j, 0, c).wait_recv()
+
+            if relayed(s):
+                pl.when(j != z)(arrive)
+            else:
+                arrive()
             return carry
 
         lax.fori_loop(0, depth, one, 0)
@@ -386,6 +417,8 @@
         for d in range(depth - 1, 0, -1):
             if 0 <= wave - d < count:
                 pass_on(wave - d, d)
+        if 0 <= wave - 1 < count and relayed(wave - 1):
+            relay(wave - 1)
         if wave + 1 < count:
             send_own(wave + 1)
         if wave < depth:
@@ -431,20 +464,15 @@
             device_id_type=MESH,
         )
 
-    def for_sib(k, block):
-        def one(p, carry):
-            to_sib[k, p] = term(block, p).astype(jnp.bfloat16)
-            sib_copy(k, p).start()
-            return carry
-
-        lax.fori_loop(0, pieces, one, 0)
-
-    def for_far(p, carry):
+    def for_sib(k, block, p):
+        to_sib[k, p] = term(block, p).astype(jnp.bfloat16)
+        sib_copy(k, p).start()
+
+    def for_far(p):
         own = term(far, p)
         sib_copy(0, p).wait_recv()
         to_far[p] = (own + from_sib[0, p].astype(jnp.float32)).astype(jnp.bfloat16)
         far_copy(p).start()
-        return carry
 
     def for_out(p, carry):
         own = term(t, p)
@@ -456,9 +484,26 @@
         ).astype(jnp.bfloat16)
         return carry
 
-    for_sib(0, (sib + 2) % 4)
-    lax.fori_loop(0, pieces, for_far, 0)
-    for_sib(1, sib)
+    lead = 2
+
+    def first_terms(p, carry):
+        @pl.when(p < pieces)
+        def _():
+            for_sib(0, (sib + 2) % 4, p)
+
+        @pl.when(p >= lead)
+        def _():
+            for_far(p - lead)
+
+        return carry
+
+    lax.fori_loop(0, pieces + lead, first_terms, 0)
+
+    def near_terms(p, carry):
+        for_sib(1, sib, p)
+        return carry
+
+    lax.fori_loop(0, pieces, near_terms, 0)
     lax.fori_loop(0, pieces, for_out, 0)
 
     def drain(p, carry):
@@ -472,7 +517,10 @@
     def drain_ctx(j, carry):
         slab = c % 2 + 2 * j
         for h in range(len(streams)):
-            ctx_copy(h, slab, 2, c).wait_send()
+            if relayed(h):
+                pl.when(j != mate)(ctx_copy(h, slab, 2, c).wait_send)
+            else:
+                ctx_copy(h, slab, 2, c).wait_send()
 
             @pl.when((j <= z) & (z < depth - 1))
             def _():
@@ -485,6 +533,10 @@
         return carry
 
     lax.fori_loop(0, depth, drain_ctx, 0)
+    for s in range(len(streams)):
+        if relayed(s):
+            pl.when(z % 2 == 0)(ctx_copy(s, other, 0, c).wait_send)
+            pl.when(z % 2 == 1)(ctx_copy(s, other, 1, c).wait_send)
 
 
 def fused_device(

time: 54.1 us -> 54.9 us (1.015)
  Pallas kernels: 52 us -> 52.8 us
    pallas_call x1, Pallas kernels: 52 us -> 52.8 us  [fused_device(): pl.pallas_call(functools.partial(fused_kernel, n), out_shape=jax.ShapeDty...]
where the time goes in v4:
time: 54.9 us; the launch traced here: 54.6 us
  Pallas kernels  52.8 us (96%)
  local copies, waits for them, and re-layouts  1.87 us (3%)
    pallas_call x1, Pallas kernels, fused_device(): pl.pallas_call(functools.partial(fused_kernel, n), out_shape=jax.ShapeDty...  52.8 us
    unnamed x1, local copies, waits for them, and re-layouts  1.87 us

profile of v4, /device:TPU:0, one launch (start us, length us, event | category | flops | bytes accessed | tf_op | source)
XLA Modules:
  0.0 54.6 jit_solution(12890911096250365637)
XLA Ops:
  0.0 52.8 %shard_map.91 = bf16[256,1024]{1,0:T(8,128)(2,1)} custom-call(bf16[128,256]{1,0:T(8,128)(2,1)} %q_hbm.1, bf16[128,256]{1,0:T(8,128)(2,1)} %k_hbm.1, bf16[128,256]{1,0:T(8,128)(2,1)} %v_hbm.1, bf16[128,256]{1,0:T(8,128)(2,1)} %o_hbm.1, bf16[128,256]{1,0:T(8,128)(2,1)} %g_hbm.1, s32[8,8]{1,0:T(8,128)} %map_ref.1, bf16[1024,256]{1,0:T(8,128)(2,1)} %wq_hbm.1, ...), custom_call_target="tpu_custom_call" | custom-call | flops 4294967296 | bytes 2097152 | tf_op jit(solution)/shard_map/pallas_call | solution.py:562
  52.8 1.9 %copy.11 = bf16[256,1024]{1,0:T(8,128)(2,1)} copy(bf16[256,1024]{1,0:T(8,128)(2,1)} %shard_map.91) | data formatting | bytes 1048576

commit v5 on v3

--- a/solution.py
+++ b/solution.py
@@ -401,7 +401,7 @@
             work(h, i)
             return carry
 
-        lax.fori_loop(0, depth, step, 0)
+        lax.fori_loop(0, depth, step, 0, unroll=2)
         if kind == 1:
             grads[:, h * HD : (h + 1) * HD] = (dq_acc[h].T * scale).astype(jnp.bfloat16)
     for copy in w_copies:

time: 54.1 us -> 53.5 us (0.989)
  Pallas kernels: 52 us -> 51.4 us
    pallas_call x1, Pallas kernels: 52 us -> 51.4 us  [fused_device(): pl.pallas_call(functools.partial(fused_kernel, n), out_shape=jax.ShapeDty...]
where the time goes in v5:
time: 53.5 us; the launch traced here: 53.3 us
  Pallas kernels  51.4 us (96%)
  local copies, waits for them, and re-layouts  1.87 us (3%)
    pallas_call x1, Pallas kernels, fused_device(): pl.pallas_call(functools.partial(fused_kernel, n), out_shape=jax.ShapeDty...  51.4 us
    unnamed x1, local copies, waits for them, and re-layouts  1.87 us

profile of v5, /device:TPU:0, one launch (start us, length us, event | category | flops | bytes accessed | tf_op | source)
XLA Modules:
  0.0 53.3 jit_solution(1921575867451917760)
XLA Ops:
  0.0 51.4 %shard_map.91 = bf16[256,1024]{1,0:T(8,128)(2,1)} custom-call(bf16[128,256]{1,0:T(8,128)(2,1)} %q_hbm.1, bf16[128,256]{1,0:T(8,128)(2,1)} %k_hbm.1, bf16[128,256]{1,0:T(8,128)(2,1)} %v_hbm.1, bf16[128,256]{1,0:T(8,128)(2,1)} %o_hbm.1, bf16[128,256]{1,0:T(8,128)(2,1)} %g_hbm.1, s32[8,8]{1,0:T(8,128)} %map_ref.1, bf16[1024,256]{1,0:T(8,128)(2,1)} %wq_hbm.1, ...), custom_call_target="tpu_custom_call" | custom-call | flops 4294967296 | bytes 2097152 | tf_op jit(solution)/shard_map/pallas_call | solution.py:510
  51.4 1.9 %copy.11 = bf16[256,1024]{1,0:T(8,128)(2,1)} copy(bf16[256,1024]{1,0:T(8,128)(2,1)} %shard_map.91) | data formatting | bytes 1048576
